TPU v7x, 128 devices: a whole 4x4x4 slice. The times are simulated.
128 devices in a mesh: freq: 32 (over y, x_hi, z), half: 4 (over x_lo, core).
Axes of the slice: x: 4 (x_hi: 2, x_lo: 2; x = x_hi * 2 + x_lo), y: 4, z: 4, core: 2. Of those that a mesh axis runs over, the one named last changes fastest.
Arguments:
- voltages: bfloat16 [4, 128, 2, 512, 1024], P('half', 'freq'), may hold values from -127 to 127
- scale_exps: int32 [4, 128, 1024], P('half', 'freq'), may hold values from 0 to 3
Outputs:
- visibilities: bfloat16 [1024, 512, 2, 1024], P('half', 'freq')
All inputs are finite; a program needn't handle non-finite values.
Results may differ from a plain program's by a relative error of at most 0.0072.
Values may be sent and summed in bfloat16 or wider, within the bound.
A program may use at most 256 MiB of HBM per device.

v0:
```python
import math

import jax
import jax.numpy as jnp
from jax import lax
from jax.sharding import PartitionSpec as P


def passed_along(block, axis, distance):
    devices = range(lax.axis_size(axis))
    route = [(i - distance, i) for i in devices if i - distance in devices]
    return lax.ppermute(block, axis, route)


def make_window(count):
    steps = jnp.arange(4 * count, dtype=jnp.float32) + 0.5
    return jnp.sinc(steps / count - 2.0) * (
        0.5 - 0.5 * jnp.cos(2.0 * math.pi * steps / (4 * count))
    )


def dft_table(count):
    index = jnp.arange(count, dtype=jnp.int32)
    angle = 2.0 * math.pi / count * (index[:, None] * index[None, :] % count).astype(jnp.float32)
    cosine = jnp.cos(angle)
    sine = jnp.sin(angle)
    upper = jnp.concatenate([cosine, sine], axis=1)
    lower = jnp.concatenate([-sine, cosine], axis=1)
    return jnp.concatenate([upper, lower], axis=0).astype(jnp.bfloat16)


def with_swapped(values):
    swapped = jnp.stack([values[:, 1], -values[:, 0]], axis=1)
    return jnp.stack([values, swapped], axis=0)


def per_device(voltages, scale_exps):
    volts = voltages[0]
    exps = scale_exps[0]
    blocks, _, count, inputs = volts.shape
    scaled = (
        volts.astype(jnp.float32) * jnp.exp2(exps.astype(jnp.float32))[:, None, None, :]
    ).astype(jnp.bfloat16)
    rims = passed_along(scaled[blocks - 3 :], "freq", 1)
    extended = jnp.concatenate([rims, scaled], axis=0)
    taps = make_window(count).reshape(4, count)
    filtered = jnp.zeros(scaled.shape, jnp.float32)
    for q in range(4):
        filtered = (
            filtered + extended[q : q + blocks].astype(jnp.float32) * taps[q][None, None, :, None]
        )
    filtered = filtered.astype(jnp.bfloat16)
    table = dft_table(count)
    spectra = jnp.einsum(
        "pq,tqi->tpi",
        table,
        filtered.reshape(blocks, 2 * count, inputs),
        preferred_element_type=jnp.float32,
    ) * (1.0 / (256.0 * math.sqrt(count)))
    spectra = spectra.reshape(blocks, 2, count, inputs).astype(jnp.bfloat16)
    turned = lax.all_to_all(spectra, "freq", split_axis=2, concat_axis=0, tiled=True)
    local_time = turned.shape[0]
    halves = lax.axis_size("half")
    weight = 1.0 / (halves * local_time)
    row_count = inputs // halves
    row_start = lax.axis_index("half") * row_count
    empty = jnp.zeros((row_count, turned.shape[2], 2, inputs), jnp.float32)
    total = empty
    piece = lax.all_gather(turned, "half", axis=0, tiled=True)
    groups = piece.shape[0] // local_time
    for group in range(groups):
        values = piece[group * local_time : (group + 1) * local_time]
        picked = lax.dynamic_slice_in_dim(values, row_start, row_count, 3)
        left = with_swapped(picked)
        part = (
            jnp.einsum("ptkcr,tkcj->rcpj", left, values, preferred_element_type=jnp.float32)
            * weight
        )
        total = total + lax.optimization_barrier(part.astype(jnp.bfloat16)).astype(jnp.float32)
    return total.astype(jnp.bfloat16)


def solution(mesh):
    return jax.shard_map(
        per_device,
        mesh=mesh,
        in_specs=(P("half", "freq", None, None, None), P("half", "freq", None)),
        out_specs=P("half", "freq", None, None),
        check_vma=False,
    )
```

profile of v0, /device:TPU:67, one launch (start us, length us, event | category | flops | bytes accessed | tf_op | source)
XLA Modules:
  0.0 782.2 jit_solution(17657897756895835511)
XLA Ops:
  6.5 0.0 all-gather.2.cloned.1.call-start
  6.5 0.7 exponential_bitcast_fusion
  7.3 9.8 %fusion.8 = bf16[4,2,512,1024]{3,2,1,0:T(8,128)(2,1)} fusion(bf16[1,4,2,512,1024]{4,3,2,1,0:T(8,128)(2,1)} %param.2, f32[4,1024]{1,0:T(4,128)S(1)} %exponential_bitcast_fusion), kind=kLoop, calls=%fused_computation.16 | loop fusion | flops 12582912 | bytes 16793600 | tf_op jit(solution)/shard_map/convert_element_type | solution.py:43
  17.1 0.0 copy-start
  17.1 3.7 slice.84
  20.8 3.6 collective-permute-start
  24.3 0.1 fusion.39
  24.4 4.0 fusion.34
  28.4 4.3 negate_convert_fusion
  32.7 126.4 %collective-permute-done = bf16[3,2,512,1024]{3,2,1,0:T(8,128)(2,1)S(1)} collective-permute-done((bf16[3,2,512,1024]{3,2,1,0:T(8,128)(2,1)S(1)}, bf16[3,2,512,1024]{3,2,1,0:T(8,128)(2,1)S(1)}, u32[]{:S(2)}, u32[]{:S(2)}) %collective-permute-start) | collective-permute-done | bytes 6291488 | tf_op jit(solution)/shard_map/ppermute | solution.py:12
  159.2 0.0 copy-start.2
  159.2 2.6 copy-done.2
  161.8 0.0 copy-done
  161.8 11.6 %add_convert_fusion.1 = bf16[4,2,512,1024]{3,2,1,0:T(8,128)(2,1)S(1)} fusion(bf16[4,2,512,1024]{3,2,1,0:T(8,128)(2,1)S(1)} %copy-done, bf16[3,2,512,1024]{3,2,1,0:T(8,128)(2,1)} %copy-done.2, f32[512]{0:T(512)S(1)} %get-tuple-element.18, f32[512]{0:T(512)S(1)} %get-tuple-element.19, f32[512]{0:T(512)S(1)} %get-tuple-element.20, f32[512]{0:T(512)S(1)} %get-tuple-element.17), kind=kLoop, calls=%fused_computation.18 | loop fusion | flops 62914560 | bytes 23076864 | tf_op jit(solution)/shard_map/convert_element_type | solution.py:52
  173.4 16.3 %multiply_convert_fusion = bf16[4,1024,1024]{1,2,0:T(8,128)(2,1)S(1)} fusion(bf16[4,1024,1024]{2,1,0:T(8,128)(2,1)S(1)} %bitcast.93, bf16[512,512]{1,0:T(8,128)(2,1)S(1)} %get-tuple-element.22, bf16[512,512]{1,0:T(8,128)(2,1)S(1)} %get-tuple-element.21, bf16[512,512]{1,0:T(8,128)(2,1)S(1)} %fusion.34), kind=kOutput, calls=%fused_computation.17 | convolution fusion | flops 8606711808 | bytes 18350080 | tf_op jit(solution)/shard_map/pq,tqi->tpi/dot_general | solution.py:54
  189.7 16.0 %copy.12 = bf16[4,2,512,1024]{3,1,0,2:T(2,128)(2,1)S(1)} copy(bf16[4,2,512,1024]{3,2,1,0:T(8,128)(2,1)S(1)} %bitcast.94) | data formatting | bytes 16777216 | tf_op jit(solution)/shard_map/convert_element_type | solution.py:60
  205.8 104.0 %all_to_all.18 = bf16[4,2,512,1024]{3,1,0,2:T(2,128)(2,1)S(1)} all-to-all(bf16[4,2,512,1024]{3,1,0,2:T(2,128)(2,1)S(1)} %copy.12), channel_id=1, replica_groups=mesh['freq'=32,'half'=4] {'freq'}, dimensions={2} | all-to-all | bytes 16777216 | tf_op jit(solution)/shard_map/all_to_all | solution.py:61
  309.8 5.6 copy.45
  315.4 12.6 %all_to_all.16 = bf16[128,2,16,1024]{3,0,1,2:T(8,128)(2,1)} reshape(bf16[32,4,2,16,1024]{4,1,0,2,3:T(4,128)(2,1)} %bitcast.92) | data formatting | bytes 16777216 | tf_op jit(solution)/shard_map/all_to_all | solution.py:61
  327.9 0.0 all-gather.2.cloned.1.call-update
  328.0 291.0 %all-gather.2.cloned.1.call-done = bf16[512,2,16,1024]{3,0,1,2:T(8,128)(2,1)} async-done(((bf16[128,2,16,1024]{3,0,1,2:T(8,128)(2,1)}), bf16[512,2,16,1024]{3,0,1,2:T(8,128)(2,1)}) %all-gather.2.cloned.1.call-update) | async-done | bytes 33554448 | tf_op jit(solution)/shard_map/all_gather | solution.py:69
  619.0 17.2 %fusion.54 = (bf16[128,2,16,1024]{3,0,1,2:T(8,128)(2,1)}, bf16[128,2,16,1024]{3,0,1,2:T(8,128)(2,1)}, bf16[128,2,16,1024]{3,0,1,2:T(8,128)(2,1)S(1)}, bf16[128,2,16,1024]{3,0,1,2:T(8,128)(2,1)S(1)}) fusion(bf16[512,2,16,1024]{3,0,1,2:T(8,128)(2,1)} %all-gather.2.cloned.1.call-done), kind=kLoop, calls=%fused_computation.105 | loop fusion | bytes 67108864 | tf_op jit(solution)/shard_map/slice | solution.py:72
  636.2 0.0 copy-start.1
  636.2 3.3 dynamic-slice_bitcast_fusion.3
  639.5 3.8 constant_dynamic-slice_fusion.3
  643.2 0.0 copy-done.1
  643.2 1.7 dynamic-slice_bitcast_fusion
  644.9 0.4 constant_dynamic-slice_fusion.1
  645.3 1.6 dynamic-slice_bitcast_fusion.1
  647.0 1.8 constant_dynamic-slice_fusion
  648.7 0.4 constant_dynamic-slice_fusion.2
  649.2 1.7 dynamic-slice_bitcast_fusion.2
  650.8 1.5 maximum_bitcast_fusion.3
  652.3 11.6 %fusion.5 = bf16[256,16,2,1024]{0,3,2,1:T(8,128)(2,1)} fusion(bf16[512,2,16,1024]{3,0,1,2:T(8,128)(2,1)} %all-gather.2.cloned.1.call-done, bf16[1,128,2,16,256]{4,1,2,3,0:T(8,128)(2,1)} %maximum_bitcast_fusion.3, bf16[1,128,2,16,256]{4,1,2,3,0:T(8,128)(2,1)} %dynamic-slice_bitcast_fusion.2), kind=kOutput, calls=%fused_computation.12 | convolution fusion | flops 4313841664 | bytes 29360128 | tf_op jit(solution)/shard_map/ptkcr,tkcj->rcpj/dot_general | solution.py:76
  663.9 3.1 maximum_bitcast_fusion.4
  666.9 11.6 %fusion.6 = bf16[256,16,2,1024]{0,3,2,1:T(8,128)(2,1)} fusion(bf16[512,2,16,1024]{3,0,1,2:T(8,128)(2,1)} %all-gather.2.cloned.1.call-done, bf16[1,128,2,16,256]{4,1,2,3,0:T(8,128)(2,1)} %maximum_bitcast_fusion.4, bf16[1,128,2,16,256]{4,1,2,3,0:T(8,128)(2,1)} %dynamic-slice_bitcast_fusion.1), kind=kOutput, calls=%fused_computation.13 | convolution fusion | flops 4313841664 | bytes 29360128 | tf_op jit(solution)/shard_map/ptkcr,tkcj->rcpj/dot_general | solution.py:76
  678.5 3.1 maximum_bitcast_fusion.2
  681.6 11.6 %fusion.4 = bf16[256,16,2,1024]{0,3,2,1:T(8,128)(2,1)} fusion(bf16[1,128,2,16,256]{4,1,2,0,3:T(8,128)(2,1)} %maximum_bitcast_fusion.2, bf16[1,128,2,16,256]{4,1,2,0,3:T(8,128)(2,1)} %dynamic-slice_bitcast_fusion.3, bf16[512,2,16,1024]{3,0,1,2:T(8,128)(2,1)} %all-gather.2.cloned.1.call-done), kind=kOutput, calls=%fused_computation.11 | convolution fusion | flops 4320133120 | bytes 29360128 | tf_op jit(solution)/shard_map/ptkcr,tkcj->rcpj/dot_general | solution.py:76
  693.2 1.5 maximum_bitcast_fusion.5
  694.7 12.0 %fusion.7 = bf16[256,16,2,1024]{0,3,2,1:T(8,128)(2,1)} fusion(bf16[512,2,16,1024]{3,0,1,2:T(8,128)(2,1)} %all-gather.2.cloned.1.call-done, bf16[1,128,2,16,256]{4,1,2,3,0:T(8,128)(2,1)} %maximum_bitcast_fusion.5, bf16[1,128,2,16,256]{4,1,2,3,0:T(8,128)(2,1)} %dynamic-slice_bitcast_fusion), kind=kOutput, calls=%fused_computation.14 | convolution fusion | flops 4313841664 | bytes 29360128 | tf_op jit(solution)/shard_map/ptkcr,tkcj->rcpj/dot_general | solution.py:76
  706.8 27.7 %add_convert_fusion = bf16[256,16,2,1024]{0,3,2,1:T(8,128)(2,1)} fusion(bf16[256,16,2,1024]{0,3,2,1:T(8,128)(2,1)} %fusion.7, bf16[256,16,2,1024]{0,3,2,1:T(8,128)(2,1)} %fusion.6, bf16[256,16,2,1024]{0,3,2,1:T(8,128)(2,1)} %fusion.5, bf16[256,16,2,1024]{0,3,2,1:T(8,128)(2,1)} %fusion.4), kind=kLoop, calls=%fused_computation.8 | loop fusion | flops 67108864 | bytes 83886080 | tf_op jit(solution)/shard_map/convert_element_type | solution.py:80
  734.5 40.9 %copy.21 = bf16[256,16,2,1024]{3,2,1,0:T(2,128)(2,1)} copy(bf16[256,16,2,1024]{0,3,2,1:T(8,128)(2,1)} %add_convert_fusion) | data formatting | bytes 33554432 | tf_op jit(solution)/shard_map/convert_element_type | solution.py:80
  (1 shorter events, 0.0 us)
Async XLA Ops:
  6.5 612.5 %all-gather.2.cloned.1.call-start = ((), (), s32[]{:S(2)}) async-start(), calls=%async_computation.1 | async-start | bytes 41943040 | tf_op jit(solution)/shard_map/all_gather | solution.py:69
  17.1 144.8 %copy-start = (bf16[4,2,512,1024]{3,2,1,0:T(8,128)(2,1)S(1)}, bf16[4,2,512,1024]{3,2,1,0:T(8,128)(2,1)}, u32[]{:S(2)}) copy-start(bf16[4,2,512,1024]{3,2,1,0:T(8,128)(2,1)} %fusion.8) | copy-start | bytes 25165828
  20.8 138.4 %collective-permute-start = (bf16[3,2,512,1024]{3,2,1,0:T(8,128)(2,1)S(1)}, bf16[3,2,512,1024]{3,2,1,0:T(8,128)(2,1)S(1)}, u32[]{:S(2)}, u32[]{:S(2)}) collective-permute-start(bf16[3,2,512,1024]{3,2,1,0:T(8,128)(2,1)S(1)} %slice.84), channel_id=1, source_target_pairs={{0,4},{4,8},{8,12},{12,16},{16,20},{20,24},{24,28},{28,32},{32,36}... | collective-permute-start | bytes 18874376 | tf_op jit(solution)/shard_map/ppermute | solution.py:12
  159.2 2.6 copy-start.2
  636.2 7.1 copy-start.1
Sparse Core Ops, SparseCore 0:
  328.1 290.8 all-gather.1
where the time goes:
time: 787 us; the launch traced here: 782 us
  waiting for transfers between devices  417 us (53%)
  local copies, waits for them, and re-layouts  107 us (14%)
  blocking collectives  104 us (13%)
  other arithmetic  73.7 us (9%)
  matrix products  63.1 us (8%)
  between operations  13.5 us (2%)
    all_gather x1, waiting for transfers between devices, per_device(): piece = lax.all_gather(turned, 'half', axis=0, tiled=True)  291 us
    ppermute x1, waiting for transfers between devices, passed_along(): return lax.ppermute(block, axis, route)  126 us
    all_to_all x1, blocking collectives, per_device(): lax.all_to_all(spectra, 'freq', split_axis=2, concat_axis=0, tiled=True)  104 us
    dot_general x4, matrix products, per_device(): jnp.einsum('ptkcr,tkcj->rcpj', left, values, preferred_element_type=jnp.f...  46.8 us
    convert_element_type x1, local copies, waits for them, and re-layouts, per_device(): return total.astype(jnp.bfloat16)  40.9 us
    convert_element_type x1, other arithmetic, per_device(): return total.astype(jnp.bfloat16)  27.7 us
    all_to_all x2, local copies, waits for them, and re-layouts, per_device(): lax.all_to_all(spectra, 'freq', split_axis=2, concat_axis=0, tiled=True)  18.1 us
    slice x1, local copies, waits for them, and re-layouts, per_device(): values = piece[group * local_time:(group + 1) * local_time]  17.2 us
  transfers between devices with their start and end apart: 2, of which 2 were waited for; matrix products, arithmetic and copies ran while one was open for 1% of the time, Pallas kernels for 0%

commit v1 on v0

v1 whole, which is shorter than its diff:
```python
import functools
import math

import jax
import jax.numpy as jnp
import ml_dtypes
import numpy as np
from jax import lax
from jax.experimental import pallas as pl
from jax.experimental.pallas import tpu as pltpu
from jax.sharding import PartitionSpec as P

MESH = pl.DeviceIdType.MESH
LANES = 128
COUNT = 512
INPUTS = 1024
CHUNKS = INPUTS // LANES
BLOCKS = 4
PEERS = 16
ROWS = 128


def make_window(count):
    steps = np.arange(4 * count, dtype=np.float64) + 0.5
    window = np.sinc(steps / count - 2.0) * (
        0.5 - 0.5 * np.cos(2.0 * math.pi * steps / (4 * count))
    )
    return window.astype(np.float32)


def dft_table(count):
    index = np.arange(count)
    angle = 2.0 * math.pi / count * (index[:, None] * index[None, :] % count)
    cosine, sine = np.cos(angle), np.sin(angle)
    upper = np.concatenate([cosine, sine], axis=1)
    lower = np.concatenate([-sine, cosine], axis=1)
    table = np.stack([upper, lower], axis=1).reshape(2 * count, 2 * count)
    return table.astype(np.float32).astype(ml_dtypes.bfloat16)


def spread_kernel(
    volts, exps, table, taps, gathered,
    local_in, left_in, right_in, exps_left, exps_right, filtered, regroup, spectra, other,
    in_sem, halo_send, halo_recv, exps_send, exps_recv, own_sem,
    peer_send, peer_recv, pass_send, pass_recv,
):
    f = lax.axis_index("freq")
    h = lax.axis_index("half")
    y, x_hi, z = f // 8, f // 4 % 2, f % 4
    x_lo = h // 2
    me = y * 4 + z
    after = {"freq": (f + 1) % 32, "half": h}
    before = {"freq": (f + 31) % 32, "half": h}
    partner = {"freq": f, "half": (h + 2) % 4}
    sibling = {"freq": f, "half": x_lo * 2 + (h + 1) % 2}
    across = {"freq": y * 8 + (1 - x_hi) * 4 + z, "half": (h + 2) % 4}

    def peer(p):
        py, pz = (y + p // 4) % 4, (z + p % 4) % 4
        return py, pz, {"freq": py * 8 + x_hi * 4 + pz, "half": h}

    def lanes(j):
        return pl.ds(pl.multiple_of(j * LANES, LANES), LANES)

    def load(j):
        return pltpu.make_async_copy(volts.at[:, :, :, lanes(j)], local_in.at[j], in_sem.at[j])

    def halo_right(j):
        return pltpu.make_async_remote_copy(
            volts.at[pl.ds(2, 2), :, :, lanes(j)], left_in.at[j],
            halo_send.at[0, j], halo_recv.at[0, j], device_id=after, device_id_type=MESH,
        )

    def halo_left(j):
        return pltpu.make_async_remote_copy(
            volts.at[pl.ds(0, 1), :, :, lanes(j)], right_in.at[j],
            halo_send.at[1, j], halo_recv.at[1, j], device_id=before, device_id_type=MESH,
        )

    def passing(kind, j, source, slot_h, slot_x, target):
        return pltpu.make_async_remote_copy(
            source, gathered.at[slot_h, slot_x, j],
            pass_send.at[kind, j], pass_recv.at[kind, j], device_id=target, device_id_type=MESH,
        )

    h2, x2 = (h + 2) % 4, 1 - x_hi
    passes = (
        lambda j: passing(0, j, gathered.at[h, x_hi, j], h, x_hi, partner),
        lambda j: passing(1, j, gathered.at[h, x_hi, j], h, x_hi, sibling),
        lambda j: passing(2, j, other.at[j], h, x_hi, across),
        lambda j: passing(3, j, gathered.at[h2, x2, j], h2, x2, partner),
        lambda j: passing(4, j, gathered.at[h2, x2, j], h2, x2, sibling),
        lambda j: passing(5, j, gathered.at[h2, x_hi, j], h2, x_hi, sibling),
        lambda j: passing(6, j, gathered.at[h, x2, j], h, x2, sibling),
    )

    barrier = pltpu.get_barrier_semaphore()

    def greet(p, carry):
        pl.semaphore_signal(barrier, inc=1, device_id=peer(p)[2], device_id_type=MESH)
        return carry

    lax.fori_loop(1, PEERS, greet, 0)
    for device in (after, before, partner, sibling, across):
        pl.semaphore_signal(barrier, inc=1, device_id=device, device_id_type=MESH)
    pl.semaphore_wait(barrier, PEERS - 1 + 5)

    exps_right_going = pltpu.make_async_remote_copy(
        exps, exps_left, exps_send.at[0], exps_recv.at[0], device_id=after, device_id_type=MESH
    )
    exps_left_going = pltpu.make_async_remote_copy(
        exps, exps_right, exps_send.at[1], exps_recv.at[1], device_id=before, device_id_type=MESH
    )
    exps_right_going.start()
    exps_left_going.start()

    def open_chunk(j, carry):
        halo_right(j).start()
        halo_left(j).start()
        load(j).start()
        return carry

    lax.fori_loop(0, CHUNKS, open_chunk, 0)
    exps_right_going.wait_recv()
    exps_left_going.wait_recv()

    not_first = jnp.where(f == 0, 0.0, 1.0).astype(jnp.float32)
    not_last = jnp.where(f == 31, 0.0, 1.0).astype(jnp.float32)

    def compute(j):
        load(j).wait()
        halo_right(j).wait_recv()
        halo_left(j).wait_recv()
        here = jnp.exp2(exps[:, lanes(j)].astype(jnp.float32))
        left = jnp.exp2(exps_left[:, lanes(j)].astype(jnp.float32)) * not_first
        right = jnp.exp2(exps_right[:, lanes(j)].astype(jnp.float32))
        factor = [left[2:3], left[3:4]] + [here[b : b + 1] for b in range(4)] + [right[0:1]]

        for k in range(2):
            def filter_rows(i, carry):
                rows = pl.ds(pl.multiple_of(i * 32, 32), 32)
                blocks = [left_in[j, b, k, rows, :] for b in range(2)]
                blocks += [local_in[j, b, k, rows, :] for b in range(4)]
                blocks += [right_in[j, 0, k, rows, :]]
                scaled = [b.astype(jnp.float32) * s for b, s in zip(blocks, factor)]
                tap = [taps[q, rows, :] for q in range(4)]
                for t in range(BLOCKS):
                    total = scaled[t] * tap[0] + scaled[t + 1] * tap[1] + scaled[t + 2] * tap[2]
                    if t == BLOCKS - 1:
                        total = total * not_last
                    total = total + scaled[t + 3] * tap[3]
                    filtered[pl.ds(pl.multiple_of(k * COUNT + i * 32, 32), 32),
                             t * LANES : (t + 1) * LANES] = total.astype(jnp.bfloat16)
                return carry

            lax.fori_loop(0, COUNT // 32, filter_rows, 0)

        def transform(m, carry):
            result = jnp.dot(
                table[pl.ds(pl.multiple_of(m * 256, 256), 256), :], filtered[...],
                preferred_element_type=jnp.float32,
            ) * (1.0 / (256.0 * math.sqrt(COUNT)))
            for t in range(BLOCKS):
                regroup[pl.ds(t, 256, stride=BLOCKS), :] = result[:, t * LANES : (t + 1) * LANES]
            spectra[j, pl.ds(m * 8, 8)] = regroup[...].astype(jnp.bfloat16).reshape(8, ROWS, LANES)
            return carry

        lax.fori_loop(0, 4, transform, 0)

    def own_copies(j):
        mine = y * 8 + x_hi * 4 + z
        rest = y * 8 + x2 * 4 + z
        return (
            pltpu.make_async_copy(spectra.at[j, mine], gathered.at[h, x_hi, j, me], own_sem.at[0, j]),
            pltpu.make_async_copy(spectra.at[j, rest], other.at[j, me], own_sem.at[1, j]),
        )

    def send_peers(j):
        for copy in own_copies(j):
            copy.start()

        def one(p, carry):
            py, pz, device = peer(p)
            pltpu.make_async_remote_copy(
                spectra.at[j, py * 8 + x_hi * 4 + pz], gathered.at[h, x_hi, j, me],
                peer_send.at[0, j], peer_recv.at[0, j], device_id=device, device_id_type=MESH,
            ).start()
            pltpu.make_async_remote_copy(
                spectra.at[j, py * 8 + x2 * 4 + pz], other.at[j, me],
                peer_send.at[1, j], peer_recv.at[1, j], device_id=device, device_id_type=MESH,
            ).start()
            return carry

        lax.fori_loop(1, PEERS, one, 0)

    def take(ref, sem):
        pltpu.make_async_copy(ref, ref, sem).wait()

    def wait_peers(j):
        for copy in own_copies(j):
            copy.wait()
        take(gathered.at[h, x_hi, j, pl.ds(0, PEERS - 1)], peer_recv.at[0, j])
        take(other.at[j, pl.ds(0, PEERS - 1)], peer_recv.at[1, j])

    def step(j, carry):
        @pl.when(j < CHUNKS)
        def _():
            compute(j)
            send_peers(j)

        @pl.when((j >= 1) & (j < CHUNKS + 1))
        def _():
            i = j - 1
            wait_peers(i)
            passes[2](i).start()
            passes[0](i).start()
            passes[1](i).start()

        @pl.when((j >= 2) & (j < CHUNKS + 2))
        def _():
            i = j - 2
            passes[2](i).wait_recv()
            passes[3](i).start()
            passes[4](i).start()
            passes[0](i).wait_recv()
            passes[5](i).start()

        @pl.when(j >= 3)
        def _():
            i = j - 3
            passes[3](i).wait_recv()
            passes[6](i).start()

        return carry

    lax.fori_loop(0, CHUNKS + 3, step, 0)

    def finish(j, carry):
        for kind in (1, 4, 5, 6):
            passes[kind](j).wait_recv()
        for kind in range(7):
            passes[kind](j).wait_send()
        halo_right(j).wait_send()
        halo_left(j).wait_send()
        take(spectra.at[j, pl.ds(0, PEERS - 1)], peer_send.at[0, j])
        take(spectra.at[j, pl.ds(0, PEERS - 1)], peer_send.at[1, j])
        return carry

    lax.fori_loop(0, CHUNKS, finish, 0)
    exps_right_going.wait_send()
    exps_left_going.wait_send()


def spread(volts, exps):
    table = jnp.asarray(dft_table(COUNT))
    taps = jnp.asarray(
        np.ascontiguousarray(
            np.broadcast_to(make_window(COUNT).reshape(4, COUNT, 1), (4, COUNT, LANES))
        )
    )
    in_vmem = pl.BlockSpec(memory_space=pltpu.VMEM)
    dma = pltpu.SemaphoreType.DMA
    return pl.pallas_call(
        spread_kernel,
        out_shape=jax.ShapeDtypeStruct((4, 2, CHUNKS, PEERS, ROWS, LANES), jnp.bfloat16),
        in_specs=[pl.BlockSpec(memory_space=pl.ANY), in_vmem, in_vmem, in_vmem],
        out_specs=pl.BlockSpec(memory_space=pl.ANY),
        scratch_shapes=[
            pltpu.VMEM((CHUNKS, BLOCKS, 2, COUNT, LANES), jnp.bfloat16),
            pltpu.VMEM((CHUNKS, 2, 2, COUNT, LANES), jnp.bfloat16),
            pltpu.VMEM((CHUNKS, 1, 2, COUNT, LANES), jnp.bfloat16),
            pltpu.VMEM((BLOCKS, INPUTS), jnp.int32),
            pltpu.VMEM((BLOCKS, INPUTS), jnp.int32),
            pltpu.VMEM((2 * COUNT, BLOCKS * LANES), jnp.bfloat16),
            pltpu.VMEM((256 * BLOCKS, LANES), jnp.float32),
            pltpu.VMEM((CHUNKS, 32, ROWS, LANES), jnp.bfloat16),
            pltpu.VMEM((CHUNKS, PEERS, ROWS, LANES), jnp.bfloat16),
            dma((CHUNKS,)),
            dma((2, CHUNKS)),
            dma((2, CHUNKS)),
            dma((2,)),
            dma((2,)),
            dma((2, CHUNKS)),
            dma((2, CHUNKS)),
            dma((2, CHUNKS)),
            dma((7, CHUNKS)),
            dma((7, CHUNKS)),
        ],
        compiler_params=pltpu.CompilerParams(
            collective_id=0, has_side_effects=True, vmem_limit_bytes=56 * 2**20
        ),
        cost_estimate=pl.CostEstimate(
            flops=8 * 2**30, bytes_accessed=50 * 2**20, transcendentals=0
        ),
    )(volts, exps, table, taps)


def correlate_kernel(spectra, out, values, left):
    half = lax.axis_index("half")
    sources = 8 * PEERS
    for u in range(CHUNKS):
        wide = spectra[:, u].astype(jnp.float32).reshape(sources, 2, 8, LANES)
        for c in range(2):
            values[c, :, u * LANES : (u + 1) * LANES] = (
                wide[:, c].reshape(sources * 8, LANES).astype(jnp.bfloat16)
            )
    sign = jnp.where(lax.broadcasted_iota(jnp.int32, (1, 8, LANES), 1) < 4, 1.0, -1.0)
    for u in range(2):
        wide = spectra[:, 2 * half + u].astype(jnp.float32).reshape(sources, 2, 8, LANES)
        for c in range(2):
            plain = wide[:, c]
            swapped = pltpu.roll(plain, 4, 1) * sign
            at = u * LANES
            left[c, :, at : at + LANES] = plain.reshape(sources * 8, LANES).astype(jnp.bfloat16)
            at = 256 + u * LANES
            left[c, :, at : at + LANES] = swapped.reshape(sources * 8, LANES).astype(jnp.bfloat16)
    for c in range(2):
        result = lax.dot_general(
            left[c], values[c], (((0,), (0,)), ((), ())), preferred_element_type=jnp.float32
        ) * (1.0 / 512.0)
        out[:, c, 0, :] = result[:256].astype(jnp.bfloat16)
        out[:, c, 1, :] = result[256:].astype(jnp.bfloat16)


def correlate(spectra):
    return pl.pallas_call(
        correlate_kernel,
        grid=(8,),
        out_shape=jax.ShapeDtypeStruct((256, 16, 2, INPUTS), jnp.bfloat16),
        in_specs=[pl.BlockSpec((8, CHUNKS, PEERS, 16, LANES), lambda i: (0, 0, 0, i, 0))],
        out_specs=pl.BlockSpec((256, 2, 2, INPUTS), lambda i: (0, i, 0, 0)),
        scratch_shapes=[
            pltpu.VMEM((2, 1024, INPUTS), jnp.bfloat16),
            pltpu.VMEM((2, 1024, 512), jnp.bfloat16),
        ],
        compiler_params=pltpu.CompilerParams(vmem_limit_bytes=56 * 2**20),
        cost_estimate=pl.CostEstimate(
            flops=16 * 2**30, bytes_accessed=48 * 2**20, transcendentals=0
        ),
    )(spectra)


def per_device(voltages, scale_exps):
    gathered = spread(voltages[0], scale_exps[0])
    return correlate(gathered.reshape(8, CHUNKS, PEERS, ROWS, LANES))


def solution(mesh):
    return jax.shard_map(
        per_device,
        mesh=mesh,
        in_specs=(P("half", "freq", None, None, None), P("half", "freq", None)),
        out_specs=P("half", "freq", None, None),
        check_vma=False,
    )
```

time: 787 us -> 343 us (0.44)
  waiting for transfers between devices: 417 us -> 0 us
  Pallas kernels: 0 us -> 342 us
  local copies, waits for them, and re-layouts: 107 us -> 0 us
  blocking collectives: 104 us -> 0 us
  other arithmetic: 73.7 us -> 0 us
  matrix products: 63.1 us -> 0 us
  between operations: 13.5 us -> 0.01 us
    pallas_call x0 -> x2, Pallas kernels: none -> 342 us  [the longest x1 312 us: spread(): pl.pallas_call(spread_kernel, out_shape=jax.ShapeDtypeStruct((4, 2, CHUNK...]
    all_gather x1 -> x0, waiting for transfers between devices: 291 us -> none  [per_device(): piece = lax.all_gather(turned, 'half', axis=0, tiled=True)]
    ppermute x1 -> x0, waiting for transfers between devices: 126 us -> none  [passed_along(): return lax.ppermute(block, axis, route)]
    all_to_all x1 -> x0, blocking collectives: 104 us -> none  [per_device(): lax.all_to_all(spectra, 'freq', split_axis=2, concat_axis=0, tiled=True)]
    dot_general x5 -> x0, matrix products: 63.1 us -> none  [the longest x4 46.8 us: per_device(): jnp.einsum('ptkcr,tkcj->rcpj', left, values, preferred_element_type=jnp.f...]
    convert_element_type x2 -> x0, local copies, waits for them, and re-layouts: 57 us -> none  [the longest x1 40.9 us: per_device(): return total.astype(jnp.bfloat16)]
    convert_element_type x3 -> x0, other arithmetic: 49.1 us -> none  [the longest x1 27.7 us: per_device(): return total.astype(jnp.bfloat16)]
    slice x3 -> x0, local copies, waits for them, and re-layouts: 20.9 us -> none  [the longest x1 17.2 us: per_device(): values = piece[group * local_time:(group + 1) * local_time]]
  transfers between devices with their start and end apart: 2 -> 0, of which waited for: 2 -> 0; matrix products, arithmetic and copies ran while one was open for 1% -> 0% of each run, Pallas kernels for 0% -> 0%
where the time goes in v1:
time: 343 us; the launch traced here: 342 us
  Pallas kernels  342 us (100%)
    pallas_call x1, Pallas kernels, spread(): pl.pallas_call(spread_kernel, out_shape=jax.ShapeDtypeStruct((4, 2, CHUNK...  312 us
    pallas_call x1, Pallas kernels, correlate(): pl.pallas_call(correlate_kernel, grid=(8,), out_shape=jax.ShapeDtypeStruc...  30.5 us

profile of v1, /device:TPU:67, one launch (start us, length us, event | category | flops | bytes accessed | tf_op | source)
XLA Modules:
  0.0 342.2 jit_solution(6201756053822864558)
XLA Ops:
  0.0 311.8 %shard_map.46 = bf16[4,2,8,16,128,128]{5,4,3,2,1,0:T(8,128)(2,1)} custom-call(bf16[4,2,512,1024]{3,2,1,0:T(8,128)(2,1)} %bitcast.4, s32[4,1024]{1,0:T(4,128)} %bitcast.5, bf16[1024,1024]{1,0:T(8,128)(2,1)} %constant.4.clone.table, f32[4,512,128]{2,1,0:T(8,128)} %constant.5.clone.taps), custom_call_target="tpu_custom_call" | custom-call | flops 8589934592 | bytes 52428800 | tf_op jit(solution)/shard_map/pallas_call | solution.py:263
  311.8 30.5 %shard_map.47 = bf16[256,16,2,1024]{3,2,1,0:T(2,128)(2,1)} custom-call(bf16[8,8,16,128,128]{4,3,2,1,0:T(8,128)(2,1)} %bitcast.3), custom_call_target="tpu_custom_call" | custom-call | flops 17179869184 | bytes 50331648 | tf_op jit(solution)/shard_map/pallas_call | solution.py:326

commit v2 on v1

--- a/solution.py
+++ b/solution.py
@@ -40,8 +40,8 @@
 
 def spread_kernel(
     volts, exps, table, taps, gathered,
-    local_in, left_in, right_in, exps_left, exps_right, filtered, regroup, spectra, other,
-    in_sem, halo_send, halo_recv, exps_send, exps_recv, own_sem,
+    window, relay, exps_left, exps_right, filtered, regroup, spectra, other,
+    in_sem, halo_send, halo_recv, relay_send, relay_recv, exps_send, exps_recv, own_sem,
     peer_send, peer_recv, pass_send, pass_recv,
 ):
     f = lax.axis_index("freq")
@@ -62,20 +62,81 @@
     def lanes(j):
         return pl.ds(pl.multiple_of(j * LANES, LANES), LANES)
 
+    wide = h % 2
+
     def load(j):
-        return pltpu.make_async_copy(volts.at[:, :, :, lanes(j)], local_in.at[j], in_sem.at[j])
-
-    def halo_right(j):
+        return pltpu.make_async_copy(
+            volts.at[:, :, :, lanes(j)], window.at[j, pl.ds(2 - wide, BLOCKS)], in_sem.at[j]
+        )
+
+    halo_block = (3, 2, 0, 1)
+
+    def place(kind, j):
+        return (1 - wide, 0, 6 - wide, 6)[kind]
+
+    def row(kind, j):
+        return (3 + j) % 4 if kind < 2 else j % 4
+
+    def halo(kind, j):
         return pltpu.make_async_remote_copy(
-            volts.at[pl.ds(2, 2), :, :, lanes(j)], left_in.at[j],
-            halo_send.at[0, j], halo_recv.at[0, j], device_id=after, device_id_type=MESH,
-        )
-
-    def halo_left(j):
+            volts.at[halo_block[kind], :, :, lanes(j)], window.at[j, place(kind, j)],
+            halo_send.at[kind, j], halo_recv.at[kind, j],
+            device_id=after if kind < 2 else before, device_id_type=MESH,
+        )
+
+    def halo_to_relay(kind, j):
         return pltpu.make_async_remote_copy(
-            volts.at[pl.ds(0, 1), :, :, lanes(j)], right_in.at[j],
-            halo_send.at[1, j], halo_recv.at[1, j], device_id=before, device_id_type=MESH,
-        )
+            volts.at[halo_block[kind], :, :, lanes(j)], relay.at[kind, j // 4],
+            halo_send.at[kind, j], relay_recv.at[kind, j // 4],
+            device_id={"freq": f - z + row(kind, j), "half": h}, device_id_type=MESH,
+        )
+
+    def halo_from_relay(kind, j):
+        beyond = (f - z + 4) % 32 if kind < 2 else (f - z + 31) % 32
+        return pltpu.make_async_remote_copy(
+            relay.at[kind, j // 4], window.at[j, place(kind, j)],
+            relay_send.at[kind, j // 4], halo_recv.at[kind, j],
+            device_id={"freq": beyond, "half": h}, device_id_type=MESH,
+        )
+
+    edge = (3, 3, 0, 0)
+
+    def each_kind(j, act):
+        for kind in range(4):
+            if kind % 2 == 0:
+                act(kind)
+            else:
+                pl.when(wide == kind // 2)(functools.partial(act, kind))
+
+    def start_halo(j):
+        def act(kind):
+            direct = (z != edge[kind]) | (row(kind, j) == edge[kind])
+            pl.when(direct)(lambda: halo(kind, j).start())
+            pl.when(jnp.logical_not(direct))(lambda: halo_to_relay(kind, j).start())
+
+        each_kind(j, act)
+
+    def relays(kind, j):
+        return (z != edge[kind]) & (row(kind, j) == z)
+
+    def relay_halo(j):
+        def act(kind):
+            @pl.when(relays(kind, j))
+            def _():
+                halo_to_relay(kind, j).wait_recv()
+                halo_from_relay(kind, j).start()
+
+        each_kind(j, act)
+
+    def wait_halo(j):
+        each_kind(j, lambda kind: halo(kind, j).wait_recv())
+
+    def finish_halo(j):
+        def act(kind):
+            halo(kind, j).wait_send()
+            pl.when(relays(kind, j))(lambda: halo_from_relay(kind, j).wait_send())
+
+        each_kind(j, act)
 
     def passing(kind, j, source, slot_h, slot_x, target):
         return pltpu.make_async_remote_copy(
@@ -103,7 +164,19 @@
     lax.fori_loop(1, PEERS, greet, 0)
     for device in (after, before, partner, sibling, across):
         pl.semaphore_signal(barrier, inc=1, device_id=device, device_id_type=MESH)
-    pl.semaphore_wait(barrier, PEERS - 1 + 5)
+    for step_back in (2, 3, 4):
+        @pl.when(z == 0)
+        def _():
+            device = {"freq": (f + 32 - step_back) % 32, "half": h}
+            pl.semaphore_signal(barrier, inc=1, device_id=device, device_id_type=MESH)
+
+        @pl.when(z == 3)
+        def _():
+            device = {"freq": (f + step_back) % 32, "half": h}
+            pl.semaphore_signal(barrier, inc=1, device_id=device, device_id_type=MESH)
+
+    edges = jnp.where(z < 3, 1, 0) + jnp.where(z > 0, 1, 0)
+    pl.semaphore_wait(barrier, PEERS - 1 + 5 + edges)
 
     exps_right_going = pltpu.make_async_remote_copy(
         exps, exps_left, exps_send.at[0], exps_recv.at[0], device_id=after, device_id_type=MESH
@@ -113,10 +186,9 @@
     )
     exps_right_going.start()
     exps_left_going.start()
+    start_halo(0)
 
     def open_chunk(j, carry):
-        halo_right(j).start()
-        halo_left(j).start()
         load(j).start()
         return carry
 
@@ -125,29 +197,32 @@
     exps_left_going.wait_recv()
 
     not_first = jnp.where(f == 0, 0.0, 1.0).astype(jnp.float32)
-    not_last = jnp.where(f == 31, 0.0, 1.0).astype(jnp.float32)
 
     def compute(j):
-        load(j).wait()
-        halo_right(j).wait_recv()
-        halo_left(j).wait_recv()
+        shift = wide
+        keep_0 = jnp.where((f == 31) & (shift == 0), 0.0, 1.0).astype(jnp.float32)
+        keep_1 = jnp.where((f == 31) & (shift == 1), 0.0, 1.0).astype(jnp.float32)
+        keep = jnp.where(f == 31, 0.0, 1.0).astype(jnp.float32)
         here = jnp.exp2(exps[:, lanes(j)].astype(jnp.float32))
         left = jnp.exp2(exps_left[:, lanes(j)].astype(jnp.float32)) * not_first
         right = jnp.exp2(exps_right[:, lanes(j)].astype(jnp.float32))
-        factor = [left[2:3], left[3:4]] + [here[b : b + 1] for b in range(4)] + [right[0:1]]
+        line = [left[2:3], left[3:4]] + [here[b : b + 1] for b in range(4)] + [right[0:1], right[1:2]]
+        factor = [jnp.where(shift == 0, line[b], line[b + 1]) for b in range(7)]
 
         for k in range(2):
             def filter_rows(i, carry):
                 rows = pl.ds(pl.multiple_of(i * 32, 32), 32)
-                blocks = [left_in[j, b, k, rows, :] for b in range(2)]
-                blocks += [local_in[j, b, k, rows, :] for b in range(4)]
-                blocks += [right_in[j, 0, k, rows, :]]
-                scaled = [b.astype(jnp.float32) * s for b, s in zip(blocks, factor)]
+                scaled = [window[j, b, k, rows, :].astype(jnp.float32) * factor[b] for b in range(7)]
                 tap = [taps[q, rows, :] for q in range(4)]
                 for t in range(BLOCKS):
-                    total = scaled[t] * tap[0] + scaled[t + 1] * tap[1] + scaled[t + 2] * tap[2]
-                    if t == BLOCKS - 1:
-                        total = total * not_last
+                    if t < 2:
+                        total = scaled[t] * tap[0] + scaled[t + 1] * tap[1] + scaled[t + 2] * tap[2]
+                    elif t == 2:
+                        total = scaled[t] * tap[0] + scaled[t + 1] * tap[1] + scaled[t + 2] * tap[2]
+                        total = total * keep_1
+                    else:
+                        total = (scaled[t] * tap[0] + scaled[t + 1] * tap[1]) * keep
+                        total = total + scaled[t + 2] * tap[2] * keep_0
                     total = total + scaled[t + 3] * tap[3]
                     filtered[pl.ds(pl.multiple_of(k * COUNT + i * 32, 32), 32),
                              t * LANES : (t + 1) * LANES] = total.astype(jnp.bfloat16)
@@ -205,8 +280,23 @@
     def step(j, carry):
         @pl.when(j < CHUNKS)
         def _():
+            load(j).wait()
+            wait_halo(j)
+
+            @pl.when(j == 0)
+            def _():
+                start_halo(1)
+
+            @pl.when(j + 2 < CHUNKS)
+            def _():
+                start_halo(j + 2)
+
             compute(j)
             send_peers(j)
+
+        @pl.when(j + 1 < CHUNKS)
+        def _():
+            relay_halo(j + 1)
 
         @pl.when((j >= 1) & (j < CHUNKS + 1))
         def _():
@@ -240,8 +330,7 @@
             passes[kind](j).wait_recv()
         for kind in range(7):
             passes[kind](j).wait_send()
-        halo_right(j).wait_send()
-        halo_left(j).wait_send()
+        finish_halo(j)
         take(spectra.at[j, pl.ds(0, PEERS - 1)], peer_send.at[0, j])
         take(spectra.at[j, pl.ds(0, PEERS - 1)], peer_send.at[1, j])
         return carry
@@ -266,9 +355,8 @@
         in_specs=[pl.BlockSpec(memory_space=pl.ANY), in_vmem, in_vmem, in_vmem],
         out_specs=pl.BlockSpec(memory_space=pl.ANY),
         scratch_shapes=[
-            pltpu.VMEM((CHUNKS, BLOCKS, 2, COUNT, LANES), jnp.bfloat16),
-            pltpu.VMEM((CHUNKS, 2, 2, COUNT, LANES), jnp.bfloat16),
-            pltpu.VMEM((CHUNKS, 1, 2, COUNT, LANES), jnp.bfloat16),
+            pltpu.VMEM((CHUNKS, 7, 2, COUNT, LANES), jnp.bfloat16),
+            pltpu.VMEM((4, 2, 2, COUNT, LANES), jnp.bfloat16),
             pltpu.VMEM((BLOCKS, INPUTS), jnp.int32),
             pltpu.VMEM((BLOCKS, INPUTS), jnp.int32),
             pltpu.VMEM((2 * COUNT, BLOCKS * LANES), jnp.bfloat16),
@@ -276,8 +364,10 @@
             pltpu.VMEM((CHUNKS, 32, ROWS, LANES), jnp.bfloat16),
             pltpu.VMEM((CHUNKS, PEERS, ROWS, LANES), jnp.bfloat16),
             dma((CHUNKS,)),
-            dma((2, CHUNKS)),
-            dma((2, CHUNKS)),
+            dma((4, CHUNKS)),
+            dma((4, CHUNKS)),
+            dma((4, 2)),
+            dma((4, 2)),
             dma((2,)),
             dma((2,)),
             dma((2, CHUNKS)),

time: 343 us -> 326 us (0.950)
  Pallas kernels: 342 us -> 326 us
    pallas_call x1, Pallas kernels: 312 us -> 295 us  [spread(): pl.pallas_call(spread_kernel, out_shape=jax.ShapeDtypeStruct((4, 2, CHUNK...]
where the time goes in v2:
time: 326 us
  Pallas kernels  326 us (100%)
    pallas_call x1, Pallas kernels, spread(): pl.pallas_call(spread_kernel, out_shape=jax.ShapeDtypeStruct((4, 2, CHUNK...  295 us
    pallas_call x1, Pallas kernels, correlate(): pl.pallas_call(correlate_kernel, grid=(8,), out_shape=jax.ShapeDtypeStruc...  30.4 us

profile of v2, /device:TPU:67, one launch (start us, length us, event | category | flops | bytes accessed | tf_op | source)
XLA Modules:
  0.0 325.9 jit_solution(3951397708630740856)
XLA Ops:
  0.0 295.4 %shard_map.46 = bf16[4,2,8,16,128,128]{5,4,3,2,1,0:T(8,128)(2,1)} custom-call(bf16[4,2,512,1024]{3,2,1,0:T(8,128)(2,1)} %bitcast.4, s32[4,1024]{1,0:T(4,128)} %bitcast.5, bf16[1024,1024]{1,0:T(8,128)(2,1)} %constant.4.clone.table, f32[4,512,128]{2,1,0:T(8,128)} %constant.5.clone.taps), custom_call_target="tpu_custom_call" | custom-call | flops 8589934592 | bytes 52428800 | tf_op jit(solution)/shard_map/pallas_call | solution.py:352
  295.4 30.4 %shard_map.47 = bf16[256,16,2,1024]{3,2,1,0:T(2,128)(2,1)} custom-call(bf16[8,8,16,128,128]{4,3,2,1,0:T(8,128)(2,1)} %bitcast.3), custom_call_target="tpu_custom_call" | custom-call | flops 17179869184 | bytes 50331648 | tf_op jit(solution)/shard_map/pallas_call | solution.py:416

commit v3 on v2

--- a/solution.py
+++ b/solution.py
@@ -74,8 +74,8 @@
     def place(kind, j):
         return (1 - wide, 0, 6 - wide, 6)[kind]
 
-    def row(kind, j):
-        return (3 + j) % 4 if kind < 2 else j % 4
+    edge = (3, 3, 0, 0)
+    part = COUNT // 4
 
     def halo(kind, j):
         return pltpu.make_async_remote_copy(
@@ -84,24 +84,30 @@
             device_id=after if kind < 2 else before, device_id_type=MESH,
         )
 
-    def halo_to_relay(kind, j):
+    def halo_part(kind, j, q):
+        rows = pl.ds(q * part, part)
+        source = volts.at[halo_block[kind], :, rows, lanes(j)]
+        if q == edge[kind]:
+            return pltpu.make_async_remote_copy(
+                source, window.at[j, place(kind, j), :, rows],
+                halo_send.at[kind, j], halo_recv.at[kind, j],
+                device_id=after if kind < 2 else before, device_id_type=MESH,
+            )
         return pltpu.make_async_remote_copy(
-            volts.at[halo_block[kind], :, :, lanes(j)], relay.at[kind, j // 4],
-            halo_send.at[kind, j], relay_recv.at[kind, j // 4],
-            device_id={"freq": f - z + row(kind, j), "half": h}, device_id_type=MESH,
+            source, relay.at[kind, j], halo_send.at[kind, j], relay_recv.at[kind, j],
+            device_id={"freq": f - z + q, "half": h}, device_id_type=MESH,
         )
 
     def halo_from_relay(kind, j):
         beyond = (f - z + 4) % 32 if kind < 2 else (f - z + 31) % 32
+        rows = pl.ds(pl.multiple_of(z * part, part), part)
         return pltpu.make_async_remote_copy(
-            relay.at[kind, j // 4], window.at[j, place(kind, j)],
-            relay_send.at[kind, j // 4], halo_recv.at[kind, j],
+            relay.at[kind, j], window.at[j, place(kind, j), :, rows],
+            relay_send.at[kind, j], halo_recv.at[kind, j],
             device_id={"freq": beyond, "half": h}, device_id_type=MESH,
         )
 
-    edge = (3, 3, 0, 0)
-
-    def each_kind(j, act):
+    def each_kind(act):
         for kind in range(4):
             if kind % 2 == 0:
                 act(kind)
@@ -110,33 +116,35 @@
 
     def start_halo(j):
         def act(kind):
-            direct = (z != edge[kind]) | (row(kind, j) == edge[kind])
-            pl.when(direct)(lambda: halo(kind, j).start())
-            pl.when(jnp.logical_not(direct))(lambda: halo_to_relay(kind, j).start())
-
-        each_kind(j, act)
-
-    def relays(kind, j):
-        return (z != edge[kind]) & (row(kind, j) == z)
+            pl.when(z != edge[kind])(lambda: halo(kind, j).start())
+
+            @pl.when(z == edge[kind])
+            def _():
+                for q in range(4):
+                    halo_part(kind, j, q).start()
+
+        each_kind(act)
 
     def relay_halo(j):
         def act(kind):
-            @pl.when(relays(kind, j))
+            @pl.when(z != edge[kind])
             def _():
-                halo_to_relay(kind, j).wait_recv()
+                pltpu.make_async_copy(
+                    relay.at[kind, j], relay.at[kind, j], relay_recv.at[kind, j]
+                ).wait()
                 halo_from_relay(kind, j).start()
 
-        each_kind(j, act)
+        each_kind(act)
 
     def wait_halo(j):
-        each_kind(j, lambda kind: halo(kind, j).wait_recv())
+        each_kind(lambda kind: halo(kind, j).wait_recv())
 
     def finish_halo(j):
         def act(kind):
             halo(kind, j).wait_send()
-            pl.when(relays(kind, j))(lambda: halo_from_relay(kind, j).wait_send())
-
-        each_kind(j, act)
+            pl.when(z != edge[kind])(lambda: halo_from_relay(kind, j).wait_send())
+
+        each_kind(act)
 
     def passing(kind, j, source, slot_h, slot_x, target):
         return pltpu.make_async_remote_copy(
@@ -187,6 +195,7 @@
     exps_right_going.start()
     exps_left_going.start()
     start_halo(0)
+    relay_halo(0)
 
     def open_chunk(j, carry):
         load(j).start()
@@ -283,20 +292,13 @@
             load(j).wait()
             wait_halo(j)
 
-            @pl.when(j == 0)
+
+            @pl.when(j + 1 < CHUNKS)
             def _():
-                start_halo(1)
-
-            @pl.when(j + 2 < CHUNKS)
-            def _():
-                start_halo(j + 2)
+                start_halo(j + 1)
 
             compute(j)
             send_peers(j)
-
-        @pl.when(j + 1 < CHUNKS)
-        def _():
-            relay_halo(j + 1)
 
         @pl.when((j >= 1) & (j < CHUNKS + 1))
         def _():
@@ -305,6 +307,10 @@
             passes[2](i).start()
             passes[0](i).start()
             passes[1](i).start()
+
+        @pl.when(j + 1 < CHUNKS)
+        def _():
+            relay_halo(j + 1)
 
         @pl.when((j >= 2) & (j < CHUNKS + 2))
         def _():
@@ -356,7 +362,7 @@
         out_specs=pl.BlockSpec(memory_space=pl.ANY),
         scratch_shapes=[
             pltpu.VMEM((CHUNKS, 7, 2, COUNT, LANES), jnp.bfloat16),
-            pltpu.VMEM((4, 2, 2, COUNT, LANES), jnp.bfloat16),
+            pltpu.VMEM((4, CHUNKS, 2, COUNT // 4, LANES), jnp.bfloat16),
             pltpu.VMEM((BLOCKS, INPUTS), jnp.int32),
             pltpu.VMEM((BLOCKS, INPUTS), jnp.int32),
             pltpu.VMEM((2 * COUNT, BLOCKS * LANES), jnp.bfloat16),
@@ -366,8 +372,8 @@
             dma((CHUNKS,)),
             dma((4, CHUNKS)),
             dma((4, CHUNKS)),
-            dma((4, 2)),
-            dma((4, 2)),
+            dma((4, CHUNKS)),
+            dma((4, CHUNKS)),
             dma((2,)),
             dma((2,)),
             dma((2, CHUNKS)),

time: 326 us -> 306 us (0.939)
  Pallas kernels: 326 us -> 304 us
    pallas_call x1, Pallas kernels: 295 us -> 274 us  [spread(): pl.pallas_call(spread_kernel, out_shape=jax.ShapeDtypeStruct((4, 2, CHUNK...]
where the time goes in v3:
time: 306 us; the launch traced here: 304 us
  Pallas kernels  304 us (99%)
    pallas_call x1, Pallas kernels, spread(): pl.pallas_call(spread_kernel, out_shape=jax.ShapeDtypeStruct((4, 2, CHUNK...  274 us
    pallas_call x1, Pallas kernels, correlate(): pl.pallas_call(correlate_kernel, grid=(8,), out_shape=jax.ShapeDtypeStruc...  30.5 us

profile of v3, /device:TPU:67, one launch (start us, length us, event | category | flops | bytes accessed | tf_op | source)
XLA Modules:
  0.0 304.3 jit_solution(5258198409708319596)
XLA Ops:
  0.0 273.8 %shard_map.46 = bf16[4,2,8,16,128,128]{5,4,3,2,1,0:T(8,128)(2,1)} custom-call(bf16[4,2,512,1024]{3,2,1,0:T(8,128)(2,1)} %bitcast.4, s32[4,1024]{1,0:T(4,128)} %bitcast.5, bf16[1024,1024]{1,0:T(8,128)(2,1)} %constant.4.clone.table, f32[4,512,128]{2,1,0:T(8,128)} %constant.5.clone.taps), custom_call_target="tpu_custom_call" | custom-call | flops 8589934592 | bytes 52428800 | tf_op jit(solution)/shard_map/pallas_call | solution.py:358
  273.8 30.5 %shard_map.47 = bf16[256,16,2,1024]{3,2,1,0:T(2,128)(2,1)} custom-call(bf16[8,8,16,128,128]{4,3,2,1,0:T(8,128)(2,1)} %bitcast.3), custom_call_target="tpu_custom_call" | custom-call | flops 17179869184 | bytes 50331648 | tf_op jit(solution)/shard_map/pallas_call | solution.py:422

commit v4 on v3

--- a/solution.py
+++ b/solution.py
@@ -266,16 +266,22 @@
         def one(p, carry):
             py, pz, device = peer(p)
             pltpu.make_async_remote_copy(
-                spectra.at[j, py * 8 + x_hi * 4 + pz], gathered.at[h, x_hi, j, me],
-                peer_send.at[0, j], peer_recv.at[0, j], device_id=device, device_id_type=MESH,
-            ).start()
-            pltpu.make_async_remote_copy(
                 spectra.at[j, py * 8 + x2 * 4 + pz], other.at[j, me],
                 peer_send.at[1, j], peer_recv.at[1, j], device_id=device, device_id_type=MESH,
             ).start()
             return carry
 
         lax.fori_loop(1, PEERS, one, 0)
+
+        def two(p, carry):
+            py, pz, device = peer(p)
+            pltpu.make_async_remote_copy(
+                spectra.at[j, py * 8 + x_hi * 4 + pz], gathered.at[h, x_hi, j, me],
+                peer_send.at[0, j], peer_recv.at[0, j], device_id=device, device_id_type=MESH,
+            ).start()
+            return carry
+
+        lax.fori_loop(1, PEERS, two, 0)
 
     def take(ref, sem):
         pltpu.make_async_copy(ref, ref, sem).wait()
@@ -297,9 +303,6 @@
             def _():
                 start_halo(j + 1)
 
-            compute(j)
-            send_peers(j)
-
         @pl.when((j >= 1) & (j < CHUNKS + 1))
         def _():
             i = j - 1
@@ -307,6 +310,11 @@
             passes[2](i).start()
             passes[0](i).start()
             passes[1](i).start()
+
+        @pl.when(j < CHUNKS)
+        def _():
+            compute(j)
+            send_peers(j)
 
         @pl.when(j + 1 < CHUNKS)
         def _():

time: 306 us -> 303 us (level)
  no operation moved by 1% of the time
where the time goes in v4:
time: 303 us; the launch traced here: 302 us
  Pallas kernels  302 us (100%)
    pallas_call x1, Pallas kernels, spread(): pl.pallas_call(spread_kernel, out_shape=jax.ShapeDtypeStruct((4, 2, CHUNK...  272 us
    pallas_call x1, Pallas kernels, correlate(): pl.pallas_call(correlate_kernel, grid=(8,), out_shape=jax.ShapeDtypeStruc...  30.5 us

profile of v4, /device:TPU:67, one launch (start us, length us, event | category | flops | bytes accessed | tf_op | source)
XLA Modules:
  0.0 302.1 jit_solution(18183201141856788685)
XLA Ops:
  0.0 271.7 %shard_map.46 = bf16[4,2,8,16,128,128]{5,4,3,2,1,0:T(8,128)(2,1)} custom-call(bf16[4,2,512,1024]{3,2,1,0:T(8,128)(2,1)} %bitcast.4, s32[4,1024]{1,0:T(4,128)} %bitcast.5, bf16[1024,1024]{1,0:T(8,128)(2,1)} %constant.4.clone.table, f32[4,512,128]{2,1,0:T(8,128)} %constant.5.clone.taps), custom_call_target="tpu_custom_call" | custom-call | flops 8589934592 | bytes 52428800 | tf_op jit(solution)/shard_map/pallas_call | solution.py:366
  271.7 30.5 %shard_map.47 = bf16[256,16,2,1024]{3,2,1,0:T(2,128)(2,1)} custom-call(bf16[8,8,16,128,128]{4,3,2,1,0:T(8,128)(2,1)} %bitcast.3), custom_call_target="tpu_custom_call" | custom-call | flops 17179869184 | bytes 50331648 | tf_op jit(solution)/shard_map/pallas_call | solution.py:430
